TPU v7x, 128 devices: a whole 4x4x4 slice. The times are simulated.
128 devices in a mesh: mp: 8 (over z, x_lo), dp: 16 (over x_hi, y, core).
Axes of the slice: x: 4 (x_hi: 2, x_lo: 2; x = x_hi * 2 + x_lo), y: 4, z: 4, core: 2. Of those that a mesh axis runs over, the one named last changes fastest.
Arguments:
- volume: bfloat16 [16, 64, 64, 2048], P('dp', 'mp'), may hold values from -6 to 6
- kernel_a: bfloat16 [3, 3, 3, 32, 64], replicated, may hold values from -0.21875 to 0.21875
- kernel_b: bfloat16 [3, 3, 3, 64, 128], P(None, None, None, 'mp'), may hold values from -0.15625 to 0.15625
- cotangent: bfloat16 [16, 16, 16, 16, 128], P('dp', None, None, None, 'mp'), may hold values from -6 to 6
Outputs:
- features: bfloat16 [16, 16, 16, 16, 128], P('dp', None, None, None, 'mp')
- grad_a: float32 [3, 3, 3, 32, 64], replicated
- grad_b: float32 [3, 3, 3, 64, 128], P(None, None, None, 'mp')
All inputs are finite; a program needn't handle non-finite values.
Results may differ from a plain program's by a relative error of at most 0.0049.
Values may be sent and summed in bfloat16 or wider, within the bound.
A program may use at most 192 MiB of HBM per device.

v0:
```python
import math
import jax
import jax.numpy as jnp
from jax import lax
from jax.sharding import PartitionSpec as P

GRID = 64


def shifted(array, axis, by):
    size = lax.axis_size(axis)
    pairs = [(i, i + by) for i in range(size) if 0 <= i + by < size]
    return lax.ppermute(array, axis, pairs)


def forward_conv(padded, kernel):
    return lax.conv_general_dilated(
        padded,
        kernel,
        (2, 2, 2),
        "VALID",
        dimension_numbers=("NDHWC", "DHWIO", "NDHWC"),
        preferred_element_type=jnp.float32,
    )


def kernel_grad(padded, grads):
    result = lax.conv_general_dilated(
        padded,
        grads,
        (1, 1, 1),
        "VALID",
        rhs_dilation=(2, 2, 2),
        dimension_numbers=("CDHWN", "IDHWO", "NDHWC"),
        preferred_element_type=jnp.float32,
    )
    return jnp.transpose(result, (1, 2, 3, 0, 4))


def input_grad(grads, kernel, first_low):
    flipped = kernel[::-1, ::-1, ::-1]
    return lax.conv_general_dilated(
        grads,
        flipped,
        (1, 1, 1),
        ((first_low, 2), (1, 2), (1, 2)),
        lhs_dilation=(2, 2, 2),
        dimension_numbers=("NDHWC", "DHWOI", "NDHWC"),
        preferred_element_type=jnp.float32,
    )


def pad_sides(field):
    return jnp.pad(field, ((0, 0), (0, 0), (1, 0), (1, 0), (0, 0)))


def pad_low(field):
    return jnp.pad(field, ((0, 0), (1, 0), (1, 0), (1, 0), (0, 0)))


def shards(volume, kernel_a, kernel_b, cotangent):
    samp_local = volume.shape[0]
    planes = volume.shape[1]
    edge = volume.shape[2]
    in_chan = kernel_a.shape[3]
    field = volume.reshape(samp_local, planes, edge, edge, in_chan)
    below = shifted(field[:, planes - 1 :], "mp", 1)
    padded_x = pad_sides(jnp.concatenate([below, field], axis=1))
    pre = forward_conv(padded_x, kernel_a)
    hidden = jnp.where(pre > 0, pre, 0.3 * pre).astype(jnp.bfloat16)
    grouped = lax.all_to_all(hidden, "mp", split_axis=4, concat_axis=1, tiled=True)
    padded_h = pad_low(grouped)
    partial_out = forward_conv(padded_h, kernel_b)
    features = lax.psum_scatter(partial_out, "mp", scatter_dimension=4, tiled=True).astype(
        jnp.bfloat16
    )
    upstream = lax.all_gather(cotangent, "mp", axis=4, tiled=True)
    local_b = kernel_grad(padded_h, upstream)
    back_group = input_grad(upstream, kernel_b, 1).astype(jnp.bfloat16)
    back = lax.all_to_all(back_group, "mp", split_axis=1, concat_axis=4, tiled=True)
    delta = (back.astype(jnp.float32) * jnp.where(pre > 0, 1.0, 0.3)).astype(jnp.bfloat16)
    local_a = kernel_grad(padded_x, delta)
    total_a = lax.psum(local_a, ("mp", "dp"))
    total_b = lax.psum(local_b, "dp")
    samples_all = samp_local * lax.axis_size("dp")
    grad_a = total_a / math.sqrt(samples_all * (GRID // 2) ** 3)
    grad_b = total_b / math.sqrt(samples_all * (GRID // 4) ** 3)
    return (features, grad_a, grad_b)


def solution(mesh):
    return jax.shard_map(
        shards,
        mesh=mesh,
        in_specs=(
            P("dp", "mp", None, None),
            P(),
            P(None, None, None, "mp", None),
            P("dp", None, None, None, "mp"),
        ),
        out_specs=(P("dp", None, None, None, "mp"), P(), P(None, None, None, "mp", None)),
        check_vma=False,
    )
```

profile of v0, /device:TPU:1, one launch (start us, length us, event | category | flops | bytes accessed | tf_op | source)
XLA Modules:
  0.0 838.3 jit_solution(7763710412680146833)
XLA Ops:
  7.2 4.9 copy.124
  14.2 4.0 collective-permute-start
  18.2 31.5 %copy.127 = bf16[1,8,64,64,32]{4,0,3,2,1:T(2,128)(2,1)} copy(bf16[1,8,64,64,32]{2,4,3,1,0:T(8,128)(2,1)} %bitcast.69) | data formatting | bytes 4194304 | tf_op jit(solution)/shard_map/reshape | solution.py:66
  52.4 58.2 %pad_maximum_fusion = bf16[1,9,64,64,32]{4,0,3,2,1:T(2,128)(2,1)} fusion(bf16[1,8,64,64,32]{4,0,3,2,1:T(2,128)(2,1)} %copy.127, bf16[1,1,64,64,32]{4,0,3,2,1:T(2,128)(2,1)S(1)} %copy.126), kind=kLoop, calls=%fused_computation.4 | loop fusion | flops 1179648 | bytes 4718592 | tf_op jit(solution)/shard_map/concatenate | solution.py:68
  110.6 33.5 %copy.128 = bf16[1,9,64,64,32]{3,4,2,1,0:T(8,128)(2,1)} copy(bf16[1,9,64,64,32]{4,0,3,2,1:T(2,128)(2,1)} %pad_maximum_fusion) | data formatting | bytes 4718592 | tf_op jit(solution)/shard_map/concatenate | solution.py:68
  144.1 9.2 %copy.159 = bf16[9,64,1,64,32]{1,4,3,0,2:T(8,128)(2,1)} copy(bf16[9,64,1,64,32]{3,4,2,1,0:T(8,128)(2,1)} %bitcast.72) | data formatting | bytes 4718592
  153.3 6.1 pad.4.clone
  159.4 15.6 %copy.131 = bf16[9,64,1,8,10,32]{5,3,4,1,0,2:T(8,128)(2,1)} copy(bf16[9,64,1,8,10,32]{1,5,4,3,0,2:T(8,128)(2,1)} %bitcast.67) | data formatting | bytes 5898240 | tf_op jit(solution)/shard_map/conv_general_dilated | solution.py:17
  177.4 12.0 %compare_select_fusion = (f32[4,32,8,5,64]{4,2,3,1,0:T(8,128)}, bf16[4,32,8,5,64]{4,2,3,1,0:T(8,128)(2,1)S(1)}) fusion(pred[8,5]{0,1:T(8,128)(4,1)S(1)} %copy-done.6, bf16[3,3,3,32,64]{4,3,2,1,0:T(8,128)(2,1)S(1)} %copy-done, bf16[9,64,1,7,2,32]{5,3,4,1,0,2:T(8,128)(2,1)S(1)} %slice.12, bf16[9,64,1,8,10,32]{5,3,4,1,0,2:T(8,128)(2,1)} %copy.131), kind=kOutput, calls=%fused_computation.20 | convolution fusion | flops 572915712 | bytes 5541928 | tf_op jit(solution)/shard_map/conv_general_dilated | solution.py:17
  195.8 6.1 all-to-all-start
  202.0 3.9 copy.140
  216.9 3.4 copy.160
  220.4 4.0 pad.6.clone
  224.4 12.8 %copy.138 = bf16[32,32,1,8,6,8]{5,3,4,1,0,2:T(8,128)(2,1)} copy(bf16[32,32,1,8,6,8]{1,5,4,3,0,2:T(8,128)(2,1)} %bitcast.73) | data formatting | bytes 1572864 | tf_op jit(solution)/shard_map/conv_general_dilated | solution.py:17
  240.6 12.3 %broadcast_select_fusion = f32[16,16,8,3,128]{4,2,3,1,0:T(8,128)S(1)} fusion(pred[8,3]{0,1:T(4,128)(4,1)S(1)} %copy-done.7, bf16[3,3,3,8,128]{4,3,2,1,0:T(8,128)(2,1)S(1)} %copy-done.5, bf16[32,32,1,7,2,8]{5,3,4,1,0,2:T(8,128)(2,1)S(1)} %slice.14, bf16[32,32,1,8,6,8]{5,3,4,1,0,2:T(8,128)(2,1)} %copy.138), kind=kOutput, calls=%fused_computation.30 | convolution fusion | flops 329662464 | bytes 4216856 | tf_op jit(solution)/shard_map/conv_general_dilated | solution.py:17
  255.2 23.8 %copy.153 = bf16[1,32,32,32,8]{4,0,3,2,1:T(2,128)(2,1)} copy(bf16[1,32,32,32,8]{3,4,2,1,0:T(8,128)(2,1)S(1)} %bitcast.71) | data formatting | bytes 1048576 | tf_op jit(solution)/shard_map/all_to_all | solution.py:71
  279.0 97.7 %all-gather.2.cloned.1.call-done = bf16[1,16,16,16,128]{3,2,1,0,4:T(8,128)(2,1)} async-done(((bf16[1,16,16,16,16]{3,2,1,0,4:T(8,128)(2,1)}), bf16[1,16,16,16,128]{3,2,1,0,4:T(8,128)(2,1)}) %all-gather.2.cloned.1.call-update) | async-done | bytes 1048592 | tf_op jit(solution)/shard_map/all_gather | solution.py:77
  376.7 10.0 %copy.141 = bf16[1,16,16,16,128]{4,3,2,1,0:T(8,128)(2,1)S(1)} copy(bf16[1,16,16,16,128]{3,2,1,0,4:T(8,128)(2,1)} %all-gather.2.cloned.1.call-done) | data formatting | bytes 2097152 | tf_op jit(solution)/shard_map/all_gather | solution.py:77
  387.9 14.3 %fusion.17 = bf16[32,32,8,6,8]{4,2,3,1,0:T(8,128)(2,1)} fusion(bf16[3,3,3,8,128]{4,3,2,1,0:T(8,128)(2,1)S(1)} %copy-done.5, bf16[16,16,1,7,1,128]{5,3,4,1,0,2:T(8,128)(2,1)S(1)} %slice.16, bf16[16,16,1,8,3,128]{5,3,4,1,0,2:T(8,128)(2,1)S(1)} %copy.144), kind=kOutput, calls=%fused_computation.24 | convolution fusion | flops 332021760 | bytes 2873344 | tf_op jit(solution)/shard_map/conv_general_dilated | solution.py:42
  402.2 13.6 %copy.145 = bf16[32,32,8,6,8]{1,4,3,2,0:T(8,128)(2,1)S(1)} copy(bf16[32,32,8,6,8]{4,2,3,1,0:T(8,128)(2,1)} %fusion.17) | data formatting | bytes 1572864 | tf_op jit(solution)/shard_map/conv_general_dilated | solution.py:42
  419.7 4.9 all-to-all-start.1
  424.6 13.5 %copy.154 = bf16[1,16,16,16,128]{4,0,3,2,1:T(2,128)(2,1)S(1)} copy(bf16[1,16,16,16,128]{3,2,1,0,4:T(8,128)(2,1)} %all-gather.2.cloned.1.call-done) | data formatting | bytes 2097152 | tf_op jit(solution)/shard_map/all_gather | solution.py:77
  438.1 51.8 %fusion.36 = f32[3,3,3,8,128]{4,3,2,1,0:T(8,128)} fusion(bf16[1,32,32,32,8]{4,0,3,2,1:T(2,128)(2,1)} %copy.153, bf16[1,16,16,16,128]{4,0,3,2,1:T(2,128)(2,1)S(1)} %copy.154), kind=kOutput, calls=%fused_computation.46 | convolution fusion | flops 212629504 | bytes 1683456 | tf_op jit(solution)/shard_map/transpose | solution.py:37
  491.3 3.4 copy.147
  494.7 3.5 fusion.12
  498.2 4.1 copy.151
  502.3 46.6 %fusion.35 = f32[3,3,3,32,64]{4,3,2,1,0:T(8,128)} fusion(bf16[1,9,64,64,32]{4,0,3,2,1:T(2,128)(2,1)} %pad_maximum_fusion, bf16[1,4,32,32,64]{4,0,3,2,1:T(2,128)(2,1)} %copy.151), kind=kOutput, calls=%fused_computation.45 | convolution fusion | flops 443596800 | bytes 3104768 | tf_op jit(solution)/shard_map/transpose | solution.py:37
  550.5 14.3 %copy.156 = f32[1,16,16,16,128]{2,3,1,0,4:T(8,128)} copy(f32[1,16,16,16,128]{4,2,3,1,0:T(8,128)} %slice_bitcast_fusion.1) | data formatting | bytes 4194304
  564.8 15.3 %reshape.69 = f32[128,4096]{1,0:T(8,128)} reshape(f32[128,1,16,16,16]{4,3,2,1,0:T(8,128)} %bitcast.66) | data formatting | bytes 4194304
  580.1 45.1 %all-reduce.5.cloned.1.call-done = f32[3,3,3,8,128]{4,3,2,1,0:T(8,128)} async-done(((f32[3,3,3,8,128]{4,3,2,1,0:T(8,128)}), f32[3,3,3,8,128]{4,3,2,1,0:T(8,128)}) %all-reduce.5.cloned.1.call-update) | async-done | bytes 110608 | tf_op jit(solution)/shard_map/psum | solution.py:84
  626.8 147.3 %all-reduce.3.cloned.1.call-done = f32[3,3,3,32,64]{4,3,2,1,0:T(8,128)} async-done(((f32[3,3,3,32,64]{4,3,2,1,0:T(8,128)}), f32[3,3,3,32,64]{4,3,2,1,0:T(8,128)}) %all-reduce.3.cloned.1.call-update) | async-done | bytes 221200 | tf_op jit(solution)/shard_map/psum | solution.py:83
  775.9 51.3 %reduce-scatter.4.cloned.1.call-done = f32[16,4096]{1,0:T(8,128)} async-done(((f32[128,4096]{1,0:T(8,128)}), f32[16,4096]{1,0:T(8,128)}) %reduce-scatter.4.cloned.1.call-update) | async-done | bytes 262160
  (57 shorter events, 46.0 us)
Async XLA Ops:
  7.2 170.2 %copy-start = (bf16[3,3,3,32,64]{4,3,2,1,0:T(8,128)(2,1)S(1)}, bf16[3,3,3,32,64]{4,3,2,1,0:T(8,128)(2,1)}, u32[]{:S(2)}) copy-start(bf16[3,3,3,32,64]{4,3,2,1,0:T(8,128)(2,1)} %param.5) | copy-start | bytes 331780
  14.2 35.5 %collective-permute-start = (bf16[1,1,64,64,32]{3,4,2,1,0:T(8,128)(2,1)S(1)}, bf16[1,1,64,64,32]{3,4,2,1,0:T(8,128)(2,1)S(1)}, u32[]{:S(2)}, u32[]{:S(2)}) collective-permute-start(bf16[1,1,64,64,32]{3,4,2,1,0:T(8,128)(2,1)S(1)} %copy.125), channel_id=1, source_target_pairs={{0,16},{16,32},{32,48},{48,64},{64,80},{80,96},{96,112},{1,17},{17... | collective-permute-start | bytes 786440 | tf_op jit(solution)/shard_map/ppermute | solution.py:13
  175.0 2.4 copy-start.6
  195.8 10.1 %copy-start.3 = (f32[4,32,8,5,64]{4,2,3,1,0:T(8,128)S(1)}, f32[4,32,8,5,64]{4,2,3,1,0:T(8,128)}, u32[]{:S(2)}) copy-start(f32[4,32,8,5,64]{4,2,3,1,0:T(8,128)} %get-tuple-element.18) | copy-start | bytes 3932164
  195.8 15.0 %all-to-all-start = ((bf16[8,2,16384]{2,1,0:T(2,128)(2,1)}), bf16[8,2,16384]{2,1,0:T(2,128)(2,1)S(1)}, u32[]{:S(2)}, u32[]{:S(2)}) async-start(bf16[8,2,16384]{2,1,0:T(2,128)(2,1)} %reshape.71), calls=%async_computation | async-start | bytes 1048576 | tf_op jit(solution)/shard_map/all_to_all | solution.py:71
  202.0 174.8 %all-gather.2.cloned.1.call-start = ((), (), s32[]{:S(2)}) async-start(), calls=%async_computation.3 | async-start | bytes 9437184 | tf_op jit(solution)/shard_map/all_gather | solution.py:77
  237.2 3.4 copy-start.5
  237.2 3.5 copy-start.7
  402.2 13.6 %copy-start.4 = (pred[8,6]{1,0:T(8,128)(4,1)S(1)}, pred[8,6]{1,0:T(8,128)(4,1)}, u32[]{:S(2)}) copy-start(pred[8,6]{1,0:T(8,128)(4,1)} %constant.31) | copy-start | bytes 148
  419.7 70.3 %all-to-all-start.1 = ((bf16[8,2,16384]{2,1,0:T(2,128)(2,1)}), bf16[8,2,16384]{2,1,0:T(2,128)(2,1)S(1)}, u32[]{:S(2)}, u32[]{:S(2)}) async-start(bf16[8,2,16384]{2,1,0:T(2,128)(2,1)} %reshape.73), calls=%async_computation.1 | async-start | bytes 1048576 | tf_op jit(solution)/shard_map/all_to_all | solution.py:80
  424.6 200.6 %all-reduce.5.cloned.1.call-start = ((), (), s32[]{:S(2)}) async-start(), calls=%async_computation.5 | async-start | bytes 221184 | tf_op jit(solution)/shard_map/psum | solution.py:84
  489.9 284.1 %all-reduce.3.cloned.1.call-start = ((), (), s32[]{:S(2)}) async-start(), calls=%async_computation.4 | async-start | bytes 884736 | tf_op jit(solution)/shard_map/psum | solution.py:83
  502.3 46.7 %copy-start.2 = (f32[16,16,8,3,128]{4,1,3,2,0:T(8,128)S(1)}, f32[16,16,8,3,128]{4,1,3,2,0:T(8,128)}, u32[]{:S(2)}) copy-start(f32[16,16,8,3,128]{4,1,3,2,0:T(8,128)} %copy.139) | copy-start | bytes 9437188
  548.9 278.3 %reduce-scatter.4.cloned.1.call-start = ((), (), s32[]{:S(2)}) async-start(), calls=%async_computation.6 | async-start | bytes 2359296
  625.2 206.2 %copy-start.1 = (bf16[3,3,3,32,64]{4,3,2,1,0:T(8,128)(2,1)S(1)}, bf16[3,3,3,32,64]{4,3,2,1,0:T(8,128)(2,1)}, u32[]{:S(2)}) copy-start(bf16[3,3,3,32,64]{4,3,2,1,0:T(8,128)(2,1)} %param.5) | copy-start | bytes 331780
Sparse Core Ops, SparseCore 0:
  206.0 170.6 all-gather.1
  490.1 135.0 all-reduce.4
  631.2 142.7 all-reduce.2
  776.3 50.8 reduce-scatter.3
where the time goes:
time: 853 us; the launch traced here: 838 us
  waiting for transfers between devices  343 us (40%)
  local copies, waits for them, and re-layouts  263 us (31%)
  matrix products  137 us (16%)
  other arithmetic  66 us (8%)
  starting transfers between devices  15.2 us (2%)
  between operations  14.4 us (2%)
    psum x1, waiting for transfers between devices, shards(): total_a = lax.psum(local_a, ('mp', 'dp'))  147 us
    transpose x2, matrix products, kernel_grad(): return jnp.transpose(result, (1, 2, 3, 0, 4))  98.3 us
    all_gather x1, waiting for transfers between devices, shards(): upstream = lax.all_gather(cotangent, 'mp', axis=4, tiled=True)  97.7 us
    unnamed x32, local copies, waits for them, and re-layouts  66.3 us
    concatenate x1, other arithmetic, shards(): padded_x = pad_sides(jnp.concatenate([below, field], axis=1))  58.2 us
    unnamed x5, waiting for transfers between devices  51.4 us
    psum x1, waiting for transfers between devices, shards(): total_b = lax.psum(local_b, 'dp')  45.1 us
    concatenate x2, local copies, waits for them, and re-layouts, shards(): padded_x = pad_sides(jnp.concatenate([below, field], axis=1))  39.5 us
  transfers between devices with their start and end apart: 7, of which 5 were waited for; matrix products, arithmetic and copies ran while one was open for 32% of the time, Pallas kernels for 0%

commit v1 on v0

--- a/solution.py
+++ b/solution.py
@@ -80,7 +80,7 @@
     back = lax.all_to_all(back_group, "mp", split_axis=1, concat_axis=4, tiled=True)
     delta = (back.astype(jnp.float32) * jnp.where(pre > 0, 1.0, 0.3)).astype(jnp.bfloat16)
     local_a = kernel_grad(padded_x, delta)
-    total_a = lax.psum(local_a, ("mp", "dp"))
+    total_a = lax.psum(lax.psum(local_a, "dp"), "mp")
     total_b = lax.psum(local_b, "dp")
     samples_all = samp_local * lax.axis_size("dp")
     grad_a = total_a / math.sqrt(samples_all * (GRID // 2) ** 3)

time: 853 us -> 736 us (0.86)
  waiting for transfers between devices: 343 us -> 228 us
    all_gather x1, waiting for transfers between devices: 97.7 us -> 0.01 us  [shards(): upstream = lax.all_gather(cotangent, 'mp', axis=4, tiled=True)]
    psum x2, waiting for transfers between devices: 192 us -> 167 us  [shards(): total_a = lax.psum(lax.psum(local_a, 'dp'), 'mp')]
    unnamed x32 -> x34, local copies, waits for them, and re-layouts: 66.3 us -> 64.8 us
  transfers between devices with their start and end apart: 7 -> 7, of which waited for: 5 -> 4; matrix products, arithmetic and copies ran while one was open for 32% -> 49% of each run, Pallas kernels for 0% -> 0%
where the time goes in v1:
time: 736 us; the launch traced here: 722 us
  local copies, waits for them, and re-layouts  264 us (36%)
  waiting for transfers between devices  228 us (31%)
  matrix products  137 us (19%)
  other arithmetic  65.1 us (9%)
  between operations  14.3 us (2%)
  starting transfers between devices  13.5 us (2%)
    psum x2, waiting for transfers between devices, shards(): total_a = lax.psum(lax.psum(local_a, 'dp'), 'mp')  167 us
    transpose x2, matrix products, kernel_grad(): return jnp.transpose(result, (1, 2, 3, 0, 4))  98.2 us
    unnamed x34, local copies, waits for them, and re-layouts  64.8 us
    concatenate x1, other arithmetic, shards(): padded_x = pad_sides(jnp.concatenate([below, field], axis=1))  58.2 us
    unnamed x5, waiting for transfers between devices  56.7 us
    concatenate x2, local copies, waits for them, and re-layouts, shards(): padded_x = pad_sides(jnp.concatenate([below, field], axis=1))  39.6 us
    conv_general_dilated x6, local copies, waits for them, and re-layouts, forward_conv(): lax.conv_general_dilated(padded, kernel, (2, 2, 2), 'VALID', dimension_nu...  38.5 us
    all_to_all x4, local copies, waits for them, and re-layouts, shards(): lax.all_to_all(hidden, 'mp', split_axis=4, concat_axis=1, tiled=True)  33.1 us
  transfers between devices with their start and end apart: 7, of which 4 were waited for; matrix products, arithmetic and copies ran while one was open for 49% of the time, Pallas kernels for 0%

profile of v1, /device:TPU:1, one launch (start us, length us, event | category | flops | bytes accessed | tf_op | source)
XLA Modules:
  0.0 722.3 jit_solution(4513401066225755487)
XLA Ops:
  7.2 4.9 copy.124
  14.3 4.0 collective-permute-start
  20.9 31.5 %copy.127 = bf16[1,8,64,64,32]{4,0,3,2,1:T(2,128)(2,1)} copy(bf16[1,8,64,64,32]{2,4,3,1,0:T(8,128)(2,1)} %bitcast.69) | data formatting | bytes 4194304 | tf_op jit(solution)/shard_map/reshape | solution.py:66
  55.0 58.2 %pad_maximum_fusion = bf16[1,9,64,64,32]{4,0,3,2,1:T(2,128)(2,1)} fusion(bf16[1,8,64,64,32]{4,0,3,2,1:T(2,128)(2,1)} %copy.127, bf16[1,1,64,64,32]{4,0,3,2,1:T(2,128)(2,1)S(1)} %copy.126), kind=kLoop, calls=%fused_computation.4 | loop fusion | flops 1179648 | bytes 4718592 | tf_op jit(solution)/shard_map/concatenate | solution.py:68
  113.2 33.6 %copy.128 = bf16[1,9,64,64,32]{3,4,2,1,0:T(8,128)(2,1)} copy(bf16[1,9,64,64,32]{4,0,3,2,1:T(2,128)(2,1)} %pad_maximum_fusion) | data formatting | bytes 4718592 | tf_op jit(solution)/shard_map/concatenate | solution.py:68
  146.8 9.2 %copy.159 = bf16[9,64,1,64,32]{1,4,3,0,2:T(8,128)(2,1)} copy(bf16[9,64,1,64,32]{3,4,2,1,0:T(8,128)(2,1)} %bitcast.72) | data formatting | bytes 4718592
  156.0 6.1 pad.4.clone
  162.1 15.6 %copy.131 = bf16[9,64,1,8,10,32]{5,3,4,1,0,2:T(8,128)(2,1)} copy(bf16[9,64,1,8,10,32]{1,5,4,3,0,2:T(8,128)(2,1)} %bitcast.67) | data formatting | bytes 5898240 | tf_op jit(solution)/shard_map/conv_general_dilated | solution.py:17
  180.1 12.0 %compare_select_fusion = (f32[4,32,8,5,64]{4,2,3,1,0:T(8,128)}, bf16[4,32,8,5,64]{4,2,3,1,0:T(8,128)(2,1)S(1)}) fusion(pred[8,5]{0,1:T(8,128)(4,1)S(1)} %copy-done.7, bf16[3,3,3,32,64]{4,3,2,1,0:T(8,128)(2,1)S(1)} %copy-done, bf16[9,64,1,7,2,32]{5,3,4,1,0,2:T(8,128)(2,1)S(1)} %slice.12, bf16[9,64,1,8,10,32]{5,3,4,1,0,2:T(8,128)(2,1)} %copy.131), kind=kOutput, calls=%fused_computation.20 | convolution fusion | flops 572915712 | bytes 5541928 | tf_op jit(solution)/shard_map/conv_general_dilated | solution.py:17
  198.7 5.9 all-to-all-start
  209.8 3.6 all-to-all-done
  219.5 3.4 copy.160
  223.0 4.0 pad.6.clone
  227.0 12.8 %copy.138 = bf16[32,32,1,8,6,8]{5,3,4,1,0,2:T(8,128)(2,1)} copy(bf16[32,32,1,8,6,8]{1,5,4,3,0,2:T(8,128)(2,1)} %bitcast.73) | data formatting | bytes 1572864 | tf_op jit(solution)/shard_map/conv_general_dilated | solution.py:17
  239.8 5.6 slice.14
  245.4 24.0 %copy.153 = bf16[1,32,32,32,8]{4,0,3,2,1:T(2,128)(2,1)} copy(bf16[1,32,32,32,8]{3,4,2,1,0:T(8,128)(2,1)S(1)} %bitcast.71) | data formatting | bytes 1048576 | tf_op jit(solution)/shard_map/all_to_all | solution.py:71
  269.4 10.0 %copy.141 = bf16[1,16,16,16,128]{4,3,2,1,0:T(8,128)(2,1)S(1)} copy(bf16[1,16,16,16,128]{3,2,1,0,4:T(8,128)(2,1)} %all-gather.2.cloned.1.call-done) | data formatting | bytes 2097152 | tf_op jit(solution)/shard_map/all_gather | solution.py:77
  280.6 14.0 %fusion.17 = bf16[32,32,8,6,8]{4,2,3,1,0:T(8,128)(2,1)} fusion(bf16[3,3,3,8,128]{4,3,2,1,0:T(8,128)(2,1)S(1)} %copy-done.5, bf16[16,16,1,7,1,128]{5,3,4,1,0,2:T(8,128)(2,1)S(1)} %slice.16, bf16[16,16,1,8,3,128]{5,3,4,1,0,2:T(8,128)(2,1)S(1)} %copy.144), kind=kOutput, calls=%fused_computation.24 | convolution fusion | flops 332021760 | bytes 2873344 | tf_op jit(solution)/shard_map/conv_general_dilated | solution.py:42
  294.6 13.6 %copy.145 = bf16[32,32,8,6,8]{1,4,3,2,0:T(8,128)(2,1)S(1)} copy(bf16[32,32,8,6,8]{4,2,3,1,0:T(8,128)(2,1)} %fusion.17) | data formatting | bytes 1572864 | tf_op jit(solution)/shard_map/conv_general_dilated | solution.py:42
  312.1 3.5 all-to-all-start.1
  315.7 13.9 %copy.154 = bf16[1,16,16,16,128]{4,0,3,2,1:T(2,128)(2,1)S(1)} copy(bf16[1,16,16,16,128]{3,2,1,0,4:T(8,128)(2,1)} %all-gather.2.cloned.1.call-done) | data formatting | bytes 2097152 | tf_op jit(solution)/shard_map/all_gather | solution.py:77
  329.6 51.8 %fusion.36 = f32[3,3,3,8,128]{4,3,2,1,0:T(8,128)} fusion(bf16[1,32,32,32,8]{4,0,3,2,1:T(2,128)(2,1)} %copy.153, bf16[1,16,16,16,128]{4,0,3,2,1:T(2,128)(2,1)S(1)} %copy.154), kind=kOutput, calls=%fused_computation.46 | convolution fusion | flops 212629504 | bytes 1683456 | tf_op jit(solution)/shard_map/transpose | solution.py:37
  382.4 3.4 copy.147
  385.9 3.5 fusion.12
  389.4 4.0 copy.151
  393.4 46.5 %fusion.35 = f32[3,3,3,32,64]{4,3,2,1,0:T(8,128)} fusion(bf16[1,9,64,64,32]{4,0,3,2,1:T(2,128)(2,1)} %pad_maximum_fusion, bf16[1,4,32,32,64]{4,0,3,2,1:T(2,128)(2,1)} %copy.151), kind=kOutput, calls=%fused_computation.45 | convolution fusion | flops 443596800 | bytes 3104768 | tf_op jit(solution)/shard_map/transpose | solution.py:37
  440.0 13.0 %broadcast_select_fusion = f32[16,16,8,3,128]{4,2,3,1,0:T(8,128)S(1)} fusion(pred[8,3]{0,1:T(4,128)(4,1)S(1)} %copy-done.8, bf16[3,3,3,8,128]{4,3,2,1,0:T(8,128)(2,1)S(1)} %copy-done.6, bf16[32,32,1,7,2,8]{5,3,4,1,0,2:T(8,128)(2,1)} %slice.14, bf16[32,32,1,8,6,8]{5,3,4,1,0,2:T(8,128)(2,1)} %copy.138), kind=kOutput, calls=%fused_computation.30 | convolution fusion | flops 329662464 | bytes 4216856 | tf_op jit(solution)/shard_map/conv_general_dilated | solution.py:17
  453.6 125.6 %all-reduce.6.cloned.1.call-done = (f32[3,3,3,32,64]{4,3,2,1,0:T(8,128)}, f32[3,3,3,8,128]{4,3,2,1,0:T(8,128)}) async-done(((f32[3,3,3,32,64]{4,3,2,1,0:T(8,128)}, f32[3,3,3,8,128]{4,3,2,1,0:T(8,128)}), (f32[3,3,3,32,64]{4,3,2,1,0:T(8,128)}, f32[3,3,3,8,128]{4,3,2,1,0:T(8,128)})) %all-reduce.6.cloned.1.call-update) | async-done | bytes 331792 | tf_op jit(solution)/shard_map/psum | solution.py:83
  580.8 14.3 %copy.156 = f32[1,16,16,16,128]{2,3,1,0,4:T(8,128)} copy(f32[1,16,16,16,128]{4,2,3,1,0:T(8,128)} %slice_bitcast_fusion.1) | data formatting | bytes 4194304
  595.0 15.3 %reshape.69 = f32[128,4096]{1,0:T(8,128)} reshape(f32[128,1,16,16,16]{4,3,2,1,0:T(8,128)} %bitcast.66) | data formatting | bytes 4194304
  611.1 41.9 %all-reduce.4.cloned.1.call-done = f32[3,3,3,32,64]{4,3,2,1,0:T(8,128)} async-done(((f32[3,3,3,32,64]{4,3,2,1,0:T(8,128)}), f32[3,3,3,32,64]{4,3,2,1,0:T(8,128)}) %all-reduce.4.cloned.1.call-update) | async-done | bytes 221200 | tf_op jit(solution)/shard_map/psum | solution.py:83
  654.8 56.6 %reduce-scatter.4.cloned.1.call-done = f32[16,4096]{1,0:T(8,128)} async-done(((f32[128,4096]{1,0:T(8,128)}), f32[16,4096]{1,0:T(8,128)}) %reduce-scatter.4.cloned.1.call-update) | async-done | bytes 262160
  (59 shorter events, 42.7 us)
Async XLA Ops:
  7.2 172.9 %copy-start = (bf16[3,3,3,32,64]{4,3,2,1,0:T(8,128)(2,1)S(1)}, bf16[3,3,3,32,64]{4,3,2,1,0:T(8,128)(2,1)}, u32[]{:S(2)}) copy-start(bf16[3,3,3,32,64]{4,3,2,1,0:T(8,128)(2,1)} %param.5) | copy-start | bytes 331780
  7.2 11.1 %copy-start.2 = (bf16[1,16,16,16,16]{4,3,2,1,0:T(8,128)(2,1)S(1)}, bf16[1,16,16,16,16]{4,3,2,1,0:T(8,128)(2,1)}, u32[]{:S(2)}) copy-start(bf16[1,16,16,16,16]{4,3,2,1,0:T(8,128)(2,1)} %param.7) | copy-start | bytes 393220
  7.2 262.2 %all-gather.2.cloned.1.call-start = ((), (), s32[]{:S(2)}) async-start(), calls=%async_computation.3 | async-start | bytes 9437184 | tf_op jit(solution)/shard_map/all_gather | solution.py:77
  14.3 38.1 %collective-permute-start = (bf16[1,1,64,64,32]{3,4,2,1,0:T(8,128)(2,1)S(1)}, bf16[1,1,64,64,32]{3,4,2,1,0:T(8,128)(2,1)S(1)}, u32[]{:S(2)}, u32[]{:S(2)}) collective-permute-start(bf16[1,1,64,64,32]{3,4,2,1,0:T(8,128)(2,1)S(1)} %copy.125), channel_id=1, source_target_pairs={{0,16},{16,32},{32,48},{48,64},{64,80},{80,96},{96,112},{1,17},{17... | collective-permute-start | bytes 786440 | tf_op jit(solution)/shard_map/ppermute | solution.py:13
  177.8 2.4 copy-start.7
  198.7 14.8 %all-to-all-start = ((bf16[8,2,16384]{2,1,0:T(2,128)(2,1)}), bf16[8,2,16384]{2,1,0:T(2,128)(2,1)S(1)}, u32[]{:S(2)}, u32[]{:S(2)}) async-start(bf16[8,2,16384]{2,1,0:T(2,128)(2,1)} %reshape.71), calls=%async_computation | async-start | bytes 1048576 | tf_op jit(solution)/shard_map/all_to_all | solution.py:71
  279.7 0.9 copy-start.5
  294.6 13.6 %copy-start.4 = (pred[8,6]{1,0:T(8,128)(4,1)S(1)}, pred[8,6]{1,0:T(8,128)(4,1)}, u32[]{:S(2)}) copy-start(pred[8,6]{1,0:T(8,128)(4,1)} %constant.31) | copy-start | bytes 148
  312.1 69.3 %all-to-all-start.1 = ((bf16[8,2,16384]{2,1,0:T(2,128)(2,1)}), bf16[8,2,16384]{2,1,0:T(2,128)(2,1)S(1)}, u32[]{:S(2)}, u32[]{:S(2)}) async-start(bf16[8,2,16384]{2,1,0:T(2,128)(2,1)} %reshape.73), calls=%async_computation.1 | async-start | bytes 1048576 | tf_op jit(solution)/shard_map/all_to_all | solution.py:80
  315.6 263.5 %all-reduce.6.cloned.1.call-start = ((), (), s32[]{:S(2)}) async-start(), calls=%async_computation.6 | async-start | bytes 1105920 | tf_op jit(solution)/shard_map/psum | solution.py:83
  393.4 46.5 %copy-start.6 = (bf16[3,3,3,8,128]{4,3,2,1,0:T(8,128)(2,1)S(1)}, bf16[3,3,3,8,128]{4,3,2,1,0:T(8,128)(2,1)}, u32[]{:S(2)}) copy-start(bf16[3,3,3,8,128]{4,3,2,1,0:T(8,128)(2,1)} %param.6) | copy-start | bytes 165892
  393.4 46.6 %copy-start.8 = (pred[8,3]{0,1:T(4,128)(4,1)S(1)}, pred[8,3]{0,1:T(4,128)(4,1)}, u32[]{:S(2)}) copy-start(pred[8,3]{0,1:T(4,128)(4,1)} %constant.29) | copy-start | bytes 76
  439.9 213.0 %all-reduce.4.cloned.1.call-start = ((), (), s32[]{:S(2)}) async-start(), calls=%async_computation.4 | async-start | bytes 884736 | tf_op jit(solution)/shard_map/psum | solution.py:83
  579.2 132.2 %reduce-scatter.4.cloned.1.call-start = ((), (), s32[]{:S(2)}) async-start(), calls=%async_computation.5 | async-start | bytes 2359296
  595.0 15.3 %copy-start.3 = (f32[3,3,3,8,128]{4,3,2,1,0:T(8,128)S(1)}, f32[3,3,3,8,128]{4,3,2,1,0:T(8,128)}, u32[]{:S(2)}) copy-start(f32[3,3,3,8,128]{4,3,2,1,0:T(8,128)} %get-tuple-element.19) | copy-start | bytes 331780
  610.4 105.2 %copy-start.1 = (bf16[3,3,3,32,64]{4,3,2,1,0:T(8,128)(2,1)S(1)}, bf16[3,3,3,32,64]{4,3,2,1,0:T(8,128)(2,1)}, u32[]{:S(2)}) copy-start(bf16[3,3,3,32,64]{4,3,2,1,0:T(8,128)(2,1)} %param.5) | copy-start | bytes 331780
Sparse Core Ops, SparseCore 0:
  21.0 170.8 all-gather.1
  440.0 139.0 all-reduce.5
  581.8 71.0 all-reduce.3
  655.2 56.1 reduce-scatter.3
